TPU v7x, 256 devices: a whole 4x4x8 slice. The times are simulated.
256 devices in a mesh: row: 4 (over y), col: 64 (over z, x, core).
Axes of the slice: x: 4, y: 4, z: 8, core: 2. Of those that a mesh axis runs over, the one named last changes fastest.
Arguments:
- amplitudes: bfloat16 [512, 512, 512], P('col', None, 'row'), may hold values from -16 to 16
- integrals: bfloat16 [512, 1, 512, 512], P(None, None, 'col', 'row'), may hold values from -0.0625 to 0.0625
- virtual_irrep: int32 [512], replicated, may hold values from 0 to 3, as said below
- pair_irrep: int32 [512], replicated, may hold values from 0 to 3, as said below
Outputs:
- residual: float32 [512, 1, 512], P('col', None, 'row')
Inputs may be any that keep to these rules, and one draw needn't show every extreme that they name: `virtual_irrep`: orbitals are sorted by irrep: labels never fall along the orbitals, and each of the 4 irreps is one contiguous run of at least 64 orbitals. `pair_irrep`: pairs are sorted by irrep: labels never fall along the pairs, and each of the 4 irreps is one contiguous run of at least 64 pairs.
All inputs are finite; a program needn't handle non-finite values.
Results may differ from a plain program's by a relative error of at most 0.0003.
Values may be sent and summed in bfloat16 or wider, within the bound.
A program may use at most 64 MiB of HBM per device.

v0:
```python
import jax
import jax.numpy as jnp
from jax import lax
from jax.sharding import PartitionSpec as P


def on_device(amplitudes, integrals, virtual_irrep, pair_irrep):
    moved = lax.all_to_all(amplitudes, "col", split_axis=1, concat_axis=0, tiled=True)
    all_pairs = moved.shape[0]
    span_d = moved.shape[1]
    span_c = moved.shape[2]
    all_b = integrals.shape[0]
    slab_a = integrals.shape[1]
    col_index = lax.axis_index("col")
    row_index = lax.axis_index("row")
    irrep_d = lax.dynamic_slice_in_dim(virtual_irrep, col_index * span_d, span_d)
    irrep_c = lax.dynamic_slice_in_dim(virtual_irrep, row_index * span_c, span_c)
    sym_dc = jnp.bitwise_xor(irrep_d[:, None], irrep_c[None, :])
    keep = pair_irrep[:, None, None] == sym_dc[None, :, :]
    masked_amp = jnp.where(keep, moved, jnp.zeros_like(moved)).reshape(all_pairs, span_d * span_c)
    b_rows = all_b // lax.axis_size("col")
    slab = integrals
    slab = slab.reshape(b_rows * lax.axis_size("col") * slab_a, span_d * span_c)
    product = lax.dot_general(
        slab, masked_amp, (((1,), (1,)), ((), ())), preferred_element_type=jnp.float32
    )
    summed = lax.psum_scatter(
        product.reshape(b_rows * lax.axis_size("col"), slab_a, all_pairs),
        "col",
        scatter_dimension=0,
        tiled=True,
    )
    result = lax.psum_scatter(summed, "row", scatter_dimension=2, tiled=True)
    pair_rows = result.shape[2]
    irrep_b = lax.dynamic_slice_in_dim(virtual_irrep, col_index * b_rows, b_rows)
    irrep_a = virtual_irrep[:slab_a]
    irrep_p = lax.dynamic_slice_in_dim(pair_irrep, row_index * pair_rows, pair_rows)
    sym_ba = jnp.bitwise_xor(irrep_b[:, None], irrep_a[None, :])
    live = sym_ba[:, :, None] == irrep_p[None, None, :]
    return jnp.where(live, result, jnp.zeros_like(result))


def solution(mesh):
    in_specs = (P("col", None, "row"), P(None, None, "col", "row"), P(), P())
    out_specs = P("col", None, "row")
    return jax.shard_map(
        on_device, mesh=mesh, in_specs=in_specs, out_specs=out_specs, check_vma=False
    )
```

profile of v0, /device:TPU:1, one launch (start us, length us, event | category | flops | bytes accessed | tf_op | source)
XLA Modules:
  0.0 267.0 jit_solution(14913951520668921622)
XLA Ops:
  6.5 2.9 %copy.11 = bf16[8,512,128]{2,0,1:T(8,128)(2,1)} copy(bf16[8,512,128]{2,1,0:T(8,128)(2,1)} %param.4) | data formatting | bytes 2097152 | tf_op args[0]
  9.4 13.1 %all-to-all-start = ((bf16[8,512,128]{2,0,1:T(8,128)(2,1)}), bf16[8,512,128]{2,0,1:T(8,128)(2,1)S(1)}, u32[]{:S(2)}, u32[]{:S(2)}) async-start(bf16[8,512,128]{2,0,1:T(8,128)(2,1)} %copy.11), calls=%async_computation | async-start | bytes 2097152 | tf_op jit(solution)/shard_map/all_to_all | solution.py:8
  22.6 0.0 all-reduce.3.cloned.1.call-start
  22.6 0.5 slice.3
  23.1 0.1 dynamic_slice.12
  23.2 0.1 eq.41
  23.3 0.7 broadcast_xor_fusion.1
  24.0 0.1 broadcast_xor_fusion
  24.1 26.4 %all-to-all-done = bf16[8,512,128]{2,0,1:T(8,128)(2,1)S(1)} async-done(((bf16[8,512,128]{2,0,1:T(8,128)(2,1)}), bf16[8,512,128]{2,0,1:T(8,128)(2,1)S(1)}, u32[]{:S(2)}, u32[]{:S(2)}) %all-to-all-start) | async-done | bytes 1048608 | tf_op jit(solution)/shard_map/all_to_all | solution.py:8
  50.5 0.7 fusion
  51.3 0.8 convolution_bitcast_fusion
  52.0 2.0 copy.13
  54.0 0.0 all-reduce.3.cloned.1.call-update
  54.0 0.0 reduce-scatter.4.cloned.1.call-start
  54.1 0.6 dynamic-slice
  55.3 179.8 %all-reduce.3.cloned.1.call-done = f32[512,1,512]{2,1,0:T(1,128)} async-done(((f32[512,1,512]{2,1,0:T(1,128)}), f32[512,1,512]{2,1,0:T(1,128)}) %all-reduce.3.cloned.1.call-update) | async-done | bytes 1048592
  235.1 0.7 constant_dynamic-slice_fusion
  235.8 0.8 copy.14
  236.6 1.3 bitcast_reduce_fusion
  237.9 0.1 dynamic_slice.11
  238.0 20.2 %reduce-scatter.4.cloned.1.call-done = f32[128,8]{1,0:T(8,128)} async-done(((f32[512,8]{1,0:T(8,128)}), f32[128,8]{1,0:T(8,128)}) %reduce-scatter.4.cloned.1.call-update) | async-done | bytes 4112
  258.2 1.0 reshape_bitcast_fusion
  259.2 0.2 copy.15
  259.4 0.7 compare_select_fusion.1
  (9 shorter events, 0.0 us)
Async XLA Ops:
  6.5 16.1 %copy-start.1 = (s32[512]{0:T(512)S(1)}, s32[512]{0:T(512)}, u32[]{:S(2)}) copy-start(s32[512]{0:T(512)} %param.6) | copy-start | bytes 6148
  6.5 16.7 %copy-start = (s32[512]{0:T(512)S(1)}, s32[512]{0:T(512)}, u32[]{:S(2)}) copy-start(s32[512]{0:T(512)} %param.7) | copy-start | bytes 6148
  9.4 41.8 %copy-start.2 = (bf16[512,1,8,128]{3,2,1,0:T(8,128)(2,1)S(1)}, bf16[512,1,8,128]{3,2,1,0:T(8,128)(2,1)}, u32[]{:S(2)}) copy-start(bf16[512,1,8,128]{3,2,1,0:T(8,128)(2,1)} %param.5) | copy-start | bytes 3145732
  9.4 41.1 %all-to-all-start = ((bf16[8,512,128]{2,0,1:T(8,128)(2,1)}), bf16[8,512,128]{2,0,1:T(8,128)(2,1)S(1)}, u32[]{:S(2)}, u32[]{:S(2)}) async-start(bf16[8,512,128]{2,0,1:T(8,128)(2,1)} %copy.11), calls=%async_computation | async-start | bytes 2097152 | tf_op jit(solution)/shard_map/all_to_all | solution.py:8
  22.6 212.5 %all-reduce.3.cloned.1.call-start = ((), (), s32[]{:S(2)}) async-start(), calls=%async_computation.3 | async-start | bytes 2097152
  52.0 2.1 copy-start.3
  54.0 204.2 %reduce-scatter.4.cloned.1.call-start = ((), (), s32[]{:S(2)}) async-start(), calls=%async_computation.2 | async-start | bytes 327680
Sparse Core Ops, SparseCore 0:
  54.1 180.9 all-reduce.2
  238.1 20.0 reduce-scatter.3
where the time goes:
time: 269 us; the launch traced here: 267 us
  waiting for transfers between devices  226 us (84%)
  between operations  14.1 us (5%)
  starting transfers between devices  13.2 us (5%)
  local copies, waits for them, and re-layouts  10.3 us (4%)
    unnamed x4, waiting for transfers between devices  200 us
    all_to_all x1, waiting for transfers between devices, on_device(): lax.all_to_all(amplitudes, 'col', split_axis=1, concat_axis=0, tiled=True)  26.4 us
    all_to_all x1, starting transfers between devices, on_device(): lax.all_to_all(amplitudes, 'col', split_axis=1, concat_axis=0, tiled=True)  13.1 us
    unnamed x15, local copies, waits for them, and re-layouts  7.55 us
  transfers between devices with their start and end apart: 3, of which 3 were waited for; matrix products, arithmetic and copies ran while one was open for 1% of the time, Pallas kernels for 0%

commit v1 on v0

v1 whole, which is shorter than its diff:
```python
import functools

import jax
import jax.numpy as jnp
from jax import lax
from jax.experimental import pallas as pl
from jax.experimental.pallas import tpu as pltpu
from jax.sharding import PartitionSpec as P

MESH = pl.DeviceIdType.MESH
F32 = jnp.float32
BF16 = jnp.bfloat16
NZ, NX, NY = 8, 4, 4
CHIPS = NZ * NX
LANES = 128
IRREPS = 4


def kernel(
    t_hbm, v_hbm, virt_ref, pair_ref, out_ref,
    recv, vbuf, vf, vmat, tf, tmat, sbuf, s1, msg, fin,
    tsend, trecv, vsem, ssend, srecv, msend, mrecv,
):
    row = lax.axis_index("row")
    col = lax.axis_index("col")
    core = lax.rem(col, 2)
    chip = lax.div(col, 2)
    z = lax.div(chip, NX)
    x = lax.rem(chip, NX)
    other = 1 - core

    def shifted(t):
        return lax.rem(z + lax.div(t, NX), NZ) * NX + lax.rem(x + lax.rem(t, NX), NX)

    def here(chip_index, core_index):
        return {"row": row, "col": chip_index * 2 + core_index}

    barrier = pltpu.get_barrier_semaphore()

    def greet(t, carry):
        pl.semaphore_signal(barrier, inc=1, device_id=here(shifted(t), core), device_id_type=MESH)
        return carry

    lax.fori_loop(1, CHIPS, greet, 0)
    pl.semaphore_signal(barrier, inc=1, device_id=here(chip, other), device_id_type=MESH)
    for hop in range(1, NY):
        for c in range(2):
            pl.semaphore_signal(
                barrier, inc=1, device_id={"row": lax.rem(row + hop, NY), "col": chip * 2 + c}, device_id_type=MESH
            )
    pl.semaphore_wait(barrier, CHIPS - 1 + 1 + 2 * (NY - 1))

    def chunk(target):
        return pltpu.make_async_remote_copy(
            src_ref=t_hbm.at[:, pl.ds(pl.multiple_of(target * 16, 16), 16), :],
            dst_ref=recv.at[chip],
            send_sem=tsend.at[target],
            recv_sem=trecv.at[chip],
            device_id=here(target, core),
            device_id_type=MESH,
        )

    def send(t, carry):
        chunk(shifted(t)).start()
        return carry

    lax.fori_loop(1, CHIPS, send, 0)
    own_t = pltpu.make_async_copy(
        t_hbm.at[:, pl.ds(pl.multiple_of(chip * 16, 16), 16), :], recv.at[chip], trecv.at[chip]
    )
    own_t.start()

    own_v = pltpu.make_async_copy(v_hbm, vbuf.at[0], vsem.at[0])
    own_v.start()
    give_v = pltpu.make_async_remote_copy(
        src_ref=v_hbm, dst_ref=vbuf.at[1], send_sem=vsem.at[1], recv_sem=vsem.at[2],
        device_id=here(chip, other), device_id_type=MESH,
    )
    give_v.start()

    labels = virt_ref[...]
    starts = []
    for n in range(1, IRREPS):
        below = jnp.where(labels < n, 1.0, 0.0).astype(F32)
        starts.append(jnp.sum(jnp.sum(below, axis=1, keepdims=True), axis=0, keepdims=True))

    def label_of(place):
        place = place.astype(F32)
        total = jnp.zeros(place.shape, jnp.int32)
        for start in starts:
            total = total + jnp.where(place >= start, 1, 0)
        return total

    irrep_a = label_of(jnp.zeros((1, LANES), jnp.int32))
    irrep_c = virt_ref[pl.ds(row, 1), :]
    irrep_b = label_of(lax.broadcasted_iota(jnp.int32, (512, LANES), 0))

    def lay_v(half, from_core):
        def widen(i, carry):
            rows = pl.ds(pl.multiple_of(i * 512, 512), 512)
            vf[rows, :] = vbuf[half, rows, :].astype(F32)
            return carry

        lax.fori_loop(0, 8, widen, 0)

        for d in range(8):
            place = chip * 16 + from_core * 8 + d
            irrep_d = label_of(jnp.full((1, LANES), 1, jnp.int32) * place)
            want = jnp.bitwise_xor(jnp.bitwise_xor(irrep_d, irrep_c), irrep_a)
            value = vf[pl.ds(d, 512, stride=8), :]
            value = jnp.where(irrep_b == want, value, 0.0)
            value = value.reshape(CHIPS, 2, 8, LANES)
            lanes = pl.ds(pl.multiple_of((from_core * 8 + d) * LANES, LANES), LANES)
            for c in range(2):
                vmat[c * 256 : c * 256 + 256, lanes] = value[:, c].reshape(256, LANES).astype(BF16)

    own_v.wait()
    lay_v(0, core)
    give_v.wait()
    lay_v(1, other)

    lane = lax.broadcasted_iota(jnp.int32, (LANES, LANES), 1)
    low = (lane < 64) == (core == 0)

    def s1_copy(q, c):
        return pltpu.make_async_remote_copy(
            src_ref=sbuf.at[q, c],
            dst_ref=s1.at[2 * row + core],
            send_sem=ssend.at[q, c],
            recv_sem=srecv.at[2 * row + core],
            device_id={"row": q, "col": chip * 2 + c},
            device_id_type=MESH,
        )

    def quarter(step, carry):
        q = lax.rem(lax.div(z, 2) + step, NY)

        def arrived(i, inner):
            source = q * 8 + i
            pltpu.make_async_copy(recv.at[source], recv.at[source], trecv.at[source]).wait()
            return inner

        lax.fori_loop(0, 8, arrived, 0)
        tf[...] = recv[pl.ds(q * 8, 8)].reshape(1024, LANES).astype(F32)
        for d in range(16):
            value = tf[pl.ds(d, 64, stride=16), :].astype(BF16)
            tmat[0:64, d * LANES : (d + 1) * LANES] = value
            tmat[64:128, d * LANES : (d + 1) * LANES] = value
        for c in range(2):
            product = lax.dot_general(
                vmat[c * 256 : c * 256 + 256, :], tmat[...], (((1,), (1,)), ((), ())), preferred_element_type=F32
            )
            packed = jnp.where(low, product[:128], product[128:])
            mine = jnp.logical_and(q == row, core == c)

            @pl.when(mine)
            def _():
                s1[2 * row + core] = packed

            @pl.when(jnp.logical_not(mine))
            def _():
                sbuf[q, c] = packed
                s1_copy(q, c).start()

        return carry

    lax.fori_loop(0, NY, quarter, 0)

    me = 2 * row + core

    def s1_wait(i, carry):
        slot = lax.rem(me + i, 8)
        pltpu.make_async_copy(s1.at[slot], s1.at[slot], srecv.at[slot]).wait()
        return carry

    lax.fori_loop(1, 8, s1_wait, 0)
    from0 = s1[0] + s1[2] + s1[4] + s1[6]
    from1 = s1[1] + s1[3] + s1[5] + s1[7]
    first = lane < 64
    msg[0:16] = jnp.where(first, from0, from1).reshape(16, 8, LANES)
    msg[16:32] = jnp.where(first, from1, from0).reshape(16, 8, LANES)

    def block(target):
        return pltpu.make_async_remote_copy(
            src_ref=msg.at[target], dst_ref=fin.at[chip], send_sem=msend.at[target], recv_sem=mrecv.at[chip],
            device_id=here(target, core), device_id_type=MESH,
        )

    def give(t, carry):
        block(shifted(t)).start()
        return carry

    lax.fori_loop(1, CHIPS, give, 0)
    fin[chip] = msg[chip]

    def taken(t, carry):
        source = shifted(t)
        pltpu.make_async_copy(fin.at[source], fin.at[source], mrecv.at[source]).wait()
        return carry

    lax.fori_loop(1, CHIPS, taken, 0)
    total = fin[0]
    for i in range(1, CHIPS):
        total = total + fin[i]

    source = lax.broadcasted_iota(jnp.int32, (LANES, LANES), 0)
    half = jnp.where(source < 64, 0, 1)
    source_core = jnp.where(chip < 16, half, 1 - half)
    inside = source - 64 * half
    target = 16 * lax.div(inside, 8) + 8 * source_core + lax.rem(inside, 8)
    move = jnp.where(target == lane, 1.0, 0.0).astype(F32)
    result = lax.dot_general(
        total, move, (((1,), (0,)), ((), ())), preferred_element_type=F32, precision=lax.Precision.HIGHEST
    )
    irrep_b8 = label_of(col * 8 + lax.broadcasted_iota(jnp.int32, (8, LANES), 0))
    live = jnp.bitwise_xor(irrep_b8, irrep_a) == pair_ref[pl.ds(row, 1), :]
    out_ref[...] = jnp.where(live, result, 0.0)

    def t_left(t, carry):
        chunk(shifted(t)).wait_send()
        block(shifted(t)).wait_send()
        return carry

    lax.fori_loop(1, CHIPS, t_left, 0)

    def s_left(i, carry):
        slot = lax.rem(me + i, 8)
        s1_copy(lax.div(slot, 2), lax.rem(slot, 2)).wait_send()
        return carry

    lax.fori_loop(1, 8, s_left, 0)


def on_device(amplitudes, integrals, virtual_irrep, pair_irrep):
    pairs, span_d, span_c = amplitudes.shape
    v = integrals.reshape(512 * 8, LANES)
    hbm = pl.BlockSpec(memory_space=pl.ANY)
    vmem = pl.BlockSpec(memory_space=pltpu.VMEM)
    out = pl.pallas_call(
        kernel,
        out_shape=jax.ShapeDtypeStruct((8, LANES), F32),
        in_specs=[hbm, hbm, vmem, vmem],
        out_specs=vmem,
        scratch_shapes=[
            pltpu.VMEM((CHIPS, 8, 16, LANES), BF16),
            pltpu.VMEM((2, 4096, LANES), BF16),
            pltpu.VMEM((4096, LANES), F32),
            pltpu.VMEM((512, 2048), BF16),
            pltpu.VMEM((1024, LANES), F32),
            pltpu.VMEM((128, 2048), BF16),
            pltpu.VMEM((4, 2, 128, LANES), F32),
            pltpu.VMEM((8, 128, LANES), F32),
            pltpu.VMEM((CHIPS, 8, LANES), F32),
            pltpu.VMEM((CHIPS, 8, LANES), F32),
            pltpu.SemaphoreType.DMA((CHIPS,)),
            pltpu.SemaphoreType.DMA((CHIPS,)),
            pltpu.SemaphoreType.DMA((3,)),
            pltpu.SemaphoreType.DMA((4, 2)),
            pltpu.SemaphoreType.DMA((8,)),
            pltpu.SemaphoreType.DMA((CHIPS,)),
            pltpu.SemaphoreType.DMA((CHIPS,)),
        ],
        compiler_params=pltpu.CompilerParams(
            collective_id=0, has_side_effects=True, vmem_limit_bytes=32 * 1024 * 1024
        ),
        name="ladder",
    )(amplitudes, v, virtual_irrep.reshape(4, LANES), pair_irrep.reshape(4, LANES))
    return out.reshape(8, 1, LANES)


def solution(mesh):
    in_specs = (P("col", None, "row"), P(None, None, "col", "row"), P(), P())
    out_specs = P("col", None, "row")
    return jax.shard_map(on_device, mesh=mesh, in_specs=in_specs, out_specs=out_specs, check_vma=False)
```

time: 269 us -> 61.1 us (0.23)
  waiting for transfers between devices: 226 us -> 0 us
  Pallas kernels: 0 us -> 57.2 us
  between operations: 14.1 us -> 0.01 us
  starting transfers between devices: 13.2 us -> 0 us
  local copies, waits for them, and re-layouts: 10.3 us -> 3.74 us
    unnamed x4 -> x0, waiting for transfers between devices: 200 us -> none
    pallas_call x0 -> x1, Pallas kernels: none -> 57.2 us  [on_device(): pl.pallas_call(kernel, out_shape=jax.ShapeDtypeStruct((8, LANES), F32), i...]
    all_to_all x1 -> x0, waiting for transfers between devices: 26.4 us -> none  [on_device(): lax.all_to_all(amplitudes, 'col', split_axis=1, concat_axis=0, tiled=True)]
    all_to_all x1 -> x0, starting transfers between devices: 13.1 us -> none  [on_device(): lax.all_to_all(amplitudes, 'col', split_axis=1, concat_axis=0, tiled=True)]
    unnamed x15 -> x9, local copies, waits for them, and re-layouts: 7.55 us -> 3.74 us
  transfers between devices with their start and end apart: 3 -> 0, of which waited for: 3 -> 0; matrix products, arithmetic and copies ran while one was open for 1% -> 0% of each run, Pallas kernels for 0% -> 0%
where the time goes in v1:
time: 61.1 us; the launch traced here: 60.9 us
  Pallas kernels  57.2 us (94%)
  local copies, waits for them, and re-layouts  3.74 us (6%)
    pallas_call x1, Pallas kernels, on_device(): pl.pallas_call(kernel, out_shape=jax.ShapeDtypeStruct((8, LANES), F32), i...  57.2 us
    unnamed x9, local copies, waits for them, and re-layouts  3.74 us

profile of v1, /device:TPU:1, one launch (start us, length us, event | category | flops | bytes accessed | tf_op | source)
XLA Modules:
  0.0 60.9 jit_solution(7591515064118429081)
XLA Ops:
  0.0 0.0 copy-start.3
  0.0 0.0 copy-start.2
  0.0 0.7 %copy-done.3 = s32[512]{0:T(512)S(1)} copy-done((s32[512]{0:T(512)S(1)}, s32[512]{0:T(512)}, u32[]{:S(2)}) %copy-start.3) | copy-done | bytes 2072
  0.7 0.0 copy-done.2
  0.7 0.0 copy-start
  0.7 1.2 %copy-done = bf16[8,512,128]{2,1,0:T(8,128)(2,1)S(1)} copy-done((bf16[8,512,128]{2,1,0:T(8,128)(2,1)S(1)}, bf16[8,512,128]{2,1,0:T(8,128)(2,1)}, u32[]{:S(2)}) %copy-start) | copy-done | bytes 1048600
  1.9 0.0 copy-start.1
  1.9 1.2 %copy-done.1 = bf16[512,1,8,128]{3,2,1,0:T(8,128)(2,1)S(1)} copy-done((bf16[512,1,8,128]{3,2,1,0:T(8,128)(2,1)S(1)}, bf16[512,1,8,128]{3,2,1,0:T(8,128)(2,1)}, u32[]{:S(2)}) %copy-start.1) | copy-done | bytes 1048600
  3.1 57.2 %ladder.1 = f32[8,128]{1,0:T(8,128)S(1)} custom-call(bf16[8,512,128]{2,1,0:T(8,128)(2,1)S(1)} %copy-done, bf16[4096,128]{1,0:T(8,128)(2,1)S(1)} %bitcast.6, s32[4,128]{1,0:T(4,128)S(1)} %bitcast.8, s32[4,128]{1,0:T(4,128)S(1)} %bitcast.9), custom_call_target="tpu_custom_call" | custom-call | tf_op jit(solution)/shard_map/ladder/pallas_call | solution.py:239
  60.3 0.6 copy.7
Async XLA Ops:
  0.0 0.7 %copy-start.3 = (s32[512]{0:T(512)S(1)}, s32[512]{0:T(512)}, u32[]{:S(2)}) copy-start(s32[512]{0:T(512)} %param.7) | copy-start | bytes 6148
  0.0 0.7 %copy-start.2 = (s32[512]{0:T(512)S(1)}, s32[512]{0:T(512)}, u32[]{:S(2)}) copy-start(s32[512]{0:T(512)} %param.6) | copy-start | bytes 6148
  0.7 1.2 %copy-start = (bf16[8,512,128]{2,1,0:T(8,128)(2,1)S(1)}, bf16[8,512,128]{2,1,0:T(8,128)(2,1)}, u32[]{:S(2)}) copy-start(bf16[8,512,128]{2,1,0:T(8,128)(2,1)} %t_hbm.1) | copy-start | bytes 3145732
  1.9 1.2 %copy-start.1 = (bf16[512,1,8,128]{3,2,1,0:T(8,128)(2,1)S(1)}, bf16[512,1,8,128]{3,2,1,0:T(8,128)(2,1)}, u32[]{:S(2)}) copy-start(bf16[512,1,8,128]{3,2,1,0:T(8,128)(2,1)} %param.5) | copy-start | bytes 3145732

commit v2 on v1

v2 whole, which is shorter than its diff:
```python
import jax
import jax.numpy as jnp
from jax import lax
from jax.experimental import pallas as pl
from jax.experimental.pallas import tpu as pltpu
from jax.sharding import PartitionSpec as P

MESH = pl.DeviceIdType.MESH
F32 = jnp.float32
BF16 = jnp.bfloat16
NZ, NX, NY = 8, 4, 4
CHIPS = NZ * NX
LANES = 128
IRREPS = 4
Z_ORDER = (4, 5, 6, 7, 2, 3, 1, 0)
X_ORDER = (2, 1, 3, 0)


def flip(value, mask, bits):
    total = 0
    for bit in range(bits):
        one = lax.rem(lax.div(value, 1 << bit), 2)
        total = total + (1 << bit) * (1 - one if mask >> bit & 1 else one)
    return total


def kernel(
    t_hbm, v_hbm, virt_hbm, pair_hbm, out_ref,
    tsrc, virt_ref, pair_ref, recv, vbuf, vf, vmat, tf, tmat, sbuf, s1, msg, fin,
    lsem, tsend, trecv, vsem, ssend, srecv, msend, mrecv,
):
    row = lax.axis_index("row")
    col = lax.axis_index("col")
    core = lax.rem(col, 2)
    chip = lax.div(col, 2)
    z = lax.div(chip, NX)
    x = lax.rem(chip, NX)
    other = 1 - core

    loads = [
        pltpu.make_async_copy(t_hbm, tsrc, lsem.at[0]),
        pltpu.make_async_copy(virt_hbm, virt_ref, lsem.at[1]),
        pltpu.make_async_copy(pair_hbm, pair_ref, lsem.at[2]),
        pltpu.make_async_copy(v_hbm, vbuf.at[0], vsem.at[0]),
    ]
    for load in loads:
        load.start()

    def around(dx):
        return lax.rem(x + dx, NX)

    def at(z_index, x_index, core_index, row_index):
        return {"row": row_index, "col": (z_index * NX + x_index) * 2 + core_index}

    plane = [(flip(z, m, 3), around(dx)) for m in Z_ORDER for dx in X_ORDER if (m, dx) != (0, 0)]
    block_mates = [(dx, dc, dy) for dy in range(NY) for dx in X_ORDER for dc in range(2)]

    barrier = pltpu.get_barrier_semaphore()
    met = 0
    for tz, tx in plane:
        pl.semaphore_signal(barrier, inc=1, device_id=at(tz, tx, core, row), device_id_type=MESH)
        met += 1
    for dx, dc, dy in block_mates:
        if dc == 0 and dy == 0:
            continue
        mate = at(z, around(dx), lax.rem(core + dc, 2), lax.rem(row + dy, NY))
        pl.semaphore_signal(barrier, inc=1, device_id=mate, device_id_type=MESH)
        met += 1
    loads[0].wait()
    pl.semaphore_wait(barrier, met)

    def chunk(tz, tx):
        target = tz * NX + tx
        return pltpu.make_async_remote_copy(
            src_ref=tsrc.at[:, pl.ds(pl.multiple_of(target * 16, 16), 16), :],
            dst_ref=recv.at[chip],
            send_sem=tsend.at[target],
            recv_sem=trecv.at[chip],
            device_id=at(tz, tx, core, row),
            device_id_type=MESH,
        )

    chunks = [chunk(tz, tx) for tz, tx in plane]
    for copy in chunks:
        copy.start()
    own_t = pltpu.make_async_copy(
        tsrc.at[:, pl.ds(pl.multiple_of(chip * 16, 16), 16), :], recv.at[chip], trecv.at[chip]
    )
    own_t.start()
    give_v = pltpu.make_async_remote_copy(
        src_ref=v_hbm, dst_ref=vbuf.at[1], send_sem=vsem.at[1], recv_sem=vsem.at[2],
        device_id=at(z, x, other, row), device_id_type=MESH,
    )
    give_v.start()

    loads[1].wait()
    loads[2].wait()
    labels = virt_ref[...]
    starts = []
    for n in range(1, IRREPS):
        below = jnp.where(labels < n, 1.0, 0.0).astype(F32)
        starts.append(jnp.sum(jnp.sum(below, axis=1, keepdims=True), axis=0, keepdims=True))

    def label_of(place):
        place = place.astype(F32)
        total = jnp.zeros(place.shape, jnp.int32)
        for start in starts:
            total = total + jnp.where(place >= start, 1, 0)
        return total

    irrep_a = label_of(jnp.zeros((1, LANES), jnp.int32))
    irrep_c = virt_ref[pl.ds(row, 1), :]
    irrep_b = label_of(lax.broadcasted_iota(jnp.int32, (512, LANES), 0))

    def lay_v(half, from_core):
        def widen(i, carry):
            rows = pl.ds(pl.multiple_of(i * 512, 512), 512)
            vf[rows, :] = vbuf[half, rows, :].astype(F32)
            return carry

        lax.fori_loop(0, 8, widen, 0)

        for d in range(8):
            place = chip * 16 + from_core * 8 + d
            irrep_d = label_of(jnp.full((1, LANES), 1, jnp.int32) * place)
            want = jnp.bitwise_xor(jnp.bitwise_xor(irrep_d, irrep_c), irrep_a)
            value = vf[pl.ds(d, 512, stride=8), :]
            value = jnp.where(irrep_b == want, value, 0.0)
            value = value.reshape(2, 4, NX, 2, 8, LANES)
            lanes = pl.ds(pl.multiple_of((from_core * 8 + d) * LANES, LANES), LANES)
            for h in range(2):
                for tx in range(NX):
                    for c in range(2):
                        at_row = h * 256 + (tx * 2 + c) * 32
                        vmat[at_row : at_row + 32, lanes] = value[h, :, tx, c].reshape(32, LANES).astype(BF16)

    loads[3].wait()
    lay_v(0, core)
    give_v.wait()
    lay_v(1, other)

    lane = lax.broadcasted_iota(jnp.int32, (256, LANES), 1)
    low = (lane < 64) == (core == 0)
    me = (row * NX + x) * 2 + core

    def s1_copy(q, tx, c):
        return pltpu.make_async_remote_copy(
            src_ref=sbuf.at[q, tx * 2 + c],
            dst_ref=s1.at[me],
            send_sem=ssend.at[q, tx * 2 + c],
            recv_sem=srecv.at[me],
            device_id=at(z, tx, c, q),
            device_id_type=MESH,
        )

    def quarter(step, carry):
        high = lax.rem(lax.div(z, 4) + 1 - lax.div(step, 2), 2)
        below = lax.rem(lax.div(z, 2) + step + lax.div(step, 2), 2)
        q = 2 * high + below

        def arrived(i, inner):
            source = q * 8 + i
            pltpu.make_async_copy(recv.at[source], recv.at[source], trecv.at[source]).wait()
            return inner

        lax.fori_loop(0, 8, arrived, 0)
        tf[...] = recv[pl.ds(q * 8, 8)].reshape(1024, LANES).astype(F32)
        for d in range(16):
            value = tf[pl.ds(d, 64, stride=16), :].astype(BF16)
            tmat[0:64, d * LANES : (d + 1) * LANES] = value
            tmat[64:128, d * LANES : (d + 1) * LANES] = value
        product = lax.dot_general(
            vmat[...], tmat[...], (((1,), (1,)), ((), ())), preferred_element_type=F32
        )
        sbuf[q] = jnp.where(low, product[:256], product[256:]).reshape(8, 32, LANES)
        for dx in X_ORDER:
            for dc in range(2):
                tx = around(dx)
                c = lax.rem(core + dc, 2)
                if (dx, dc) == (0, 0):

                    @pl.when(q == row)
                    def _():
                        s1[me] = sbuf[q, tx * 2 + c]

                    @pl.when(q != row)
                    def _():
                        s1_copy(q, tx, c).start()

                else:
                    s1_copy(q, tx, c).start()
        return carry

    lax.fori_loop(0, NY, quarter, 0)

    def s1_wait(i, carry):
        slot = lax.rem(me + i, 32)
        pltpu.make_async_copy(s1.at[slot], s1.at[slot], srecv.at[slot]).wait()
        return carry

    lax.fori_loop(1, 32, s1_wait, 0)
    from0, from1 = s1[0], s1[1]
    for i in range(2, 32, 2):
        from0 = from0 + s1[i]
        from1 = from1 + s1[i + 1]
    first = lax.broadcasted_iota(jnp.int32, (32, LANES), 1) < 64
    msg[0:4] = jnp.where(first, from0, from1).reshape(4, 8, LANES)
    msg[4:8] = jnp.where(first, from1, from0).reshape(4, 8, LANES)

    def block(tz):
        return pltpu.make_async_remote_copy(
            src_ref=msg.at[tz], dst_ref=fin.at[z], send_sem=msend.at[tz], recv_sem=mrecv.at[z],
            device_id=at(tz, x, core, row), device_id_type=MESH,
        )

    blocks = [block(lax.rem(z + dz, NZ)) for dz in (4, 3, 5, 2, 6, 1, 7)]
    for copy in blocks:
        copy.start()
    fin[z] = msg[z]
    for dz in (1, 7, 2, 6, 3, 5, 4):
        source = lax.rem(z + dz, NZ)
        pltpu.make_async_copy(fin.at[source], fin.at[source], mrecv.at[source]).wait()
    total = fin[0]
    for i in range(1, NZ):
        total = total + fin[i]

    source = lax.broadcasted_iota(jnp.int32, (LANES, LANES), 0)
    target_lane = lax.broadcasted_iota(jnp.int32, (LANES, LANES), 1)
    half = jnp.where(source < 64, 0, 1)
    source_core = jnp.where(z < 4, half, 1 - half)
    inside = source - 64 * half
    target = 16 * lax.div(inside, 8) + 8 * source_core + lax.rem(inside, 8)
    move = jnp.where(target == target_lane, 1.0, 0.0).astype(F32)
    result = lax.dot_general(
        total, move, (((1,), (0,)), ((), ())), preferred_element_type=F32, precision=lax.Precision.HIGHEST
    )
    irrep_b8 = label_of(col * 8 + lax.broadcasted_iota(jnp.int32, (8, LANES), 0))
    live = jnp.bitwise_xor(irrep_b8, irrep_a) == pair_ref[pl.ds(row, 1), :]
    out_ref[...] = jnp.where(live, result, 0.0)

    for copy in chunks + blocks:
        copy.wait_send()

    def s_left(i, carry):
        slot = lax.rem(me + i, 32)
        s1_copy(lax.div(slot, 8), lax.div(lax.rem(slot, 8), 2), lax.rem(slot, 2)).wait_send()
        return carry

    lax.fori_loop(1, 32, s_left, 0)


def on_device(amplitudes, integrals, virtual_irrep, pair_irrep):
    v = integrals.reshape(512 * 8, LANES)
    hbm = pl.BlockSpec(memory_space=pltpu.HBM)
    out = pl.pallas_call(
        kernel,
        out_shape=jax.ShapeDtypeStruct((8, LANES), F32),
        in_specs=[hbm, hbm, hbm, hbm],
        out_specs=pl.BlockSpec(memory_space=pltpu.VMEM),
        scratch_shapes=[
            pltpu.VMEM((8, 512, LANES), BF16),
            pltpu.VMEM((4, LANES), jnp.int32),
            pltpu.VMEM((4, LANES), jnp.int32),
            pltpu.VMEM((CHIPS, 8, 16, LANES), BF16),
            pltpu.VMEM((2, 4096, LANES), BF16),
            pltpu.VMEM((4096, LANES), F32),
            pltpu.VMEM((512, 2048), BF16),
            pltpu.VMEM((1024, LANES), F32),
            pltpu.VMEM((128, 2048), BF16),
            pltpu.VMEM((4, 8, 32, LANES), F32),
            pltpu.VMEM((32, 32, LANES), F32),
            pltpu.VMEM((8, 8, LANES), F32),
            pltpu.VMEM((8, 8, LANES), F32),
            pltpu.SemaphoreType.DMA((3,)),
            pltpu.SemaphoreType.DMA((CHIPS,)),
            pltpu.SemaphoreType.DMA((CHIPS,)),
            pltpu.SemaphoreType.DMA((3,)),
            pltpu.SemaphoreType.DMA((4, 8)),
            pltpu.SemaphoreType.DMA((32,)),
            pltpu.SemaphoreType.DMA((NZ,)),
            pltpu.SemaphoreType.DMA((NZ,)),
        ],
        compiler_params=pltpu.CompilerParams(
            collective_id=0, has_side_effects=True, vmem_limit_bytes=63 * 1024 * 1024
        ),
        name="ladder",
    )(amplitudes, v, virtual_irrep.reshape(4, LANES), pair_irrep.reshape(4, LANES))
    return out.reshape(8, 1, LANES)


def solution(mesh):
    in_specs = (P("col", None, "row"), P(None, None, "col", "row"), P(), P())
    out_specs = P("col", None, "row")
    return jax.shard_map(on_device, mesh=mesh, in_specs=in_specs, out_specs=out_specs, check_vma=False)
```

time: 61.1 us -> 52.3 us (0.86)
  Pallas kernels: 57.2 us -> 50.9 us
  local copies, waits for them, and re-layouts: 3.74 us -> 1.28 us
    pallas_call x1, Pallas kernels: 57.2 us -> 50.9 us  [on_device(): pl.pallas_call(kernel, out_shape=jax.ShapeDtypeStruct((8, LANES), F32), i...]
    unnamed x9 -> x1, local copies, waits for them, and re-layouts: 3.74 us -> 1.28 us
where the time goes in v2:
time: 52.3 us; the launch traced here: 52.2 us
  Pallas kernels  50.9 us (97%)
  local copies, waits for them, and re-layouts  1.28 us (2%)
    pallas_call x1, Pallas kernels, on_device(): pl.pallas_call(kernel, out_shape=jax.ShapeDtypeStruct((8, LANES), F32), i...  50.9 us
    unnamed x1, local copies, waits for them, and re-layouts  1.28 us

profile of v2, /device:TPU:1, one launch (start us, length us, event | category | flops | bytes accessed | tf_op | source)
XLA Modules:
  0.0 52.2 jit_solution(8383490607903684260)
XLA Ops:
  0.0 50.9 %ladder.1 = f32[8,128]{1,0:T(8,128)} custom-call(bf16[8,512,128]{2,1,0:T(8,128)(2,1)} %t_hbm.1, bf16[4096,128]{1,0:T(8,128)(2,1)} %bitcast.6, s32[4,128]{1,0:T(4,128)} %bitcast.8, s32[4,128]{1,0:T(4,128)} %bitcast.9), custom_call_target="tpu_custom_call" | custom-call | tf_op jit(solution)/shard_map/ladder/pallas_call | solution.py:255
  50.9 1.3 %copy.7 = f32[8,1,128]{2,1,0:T(1,128)} copy(f32[8,1,128]{2,1,0:T(1,128)} %bitcast.7) | data formatting | bytes 8192

commit v3 on v2

v3 whole, which is shorter than its diff:
```python
import jax
import jax.numpy as jnp
from jax import lax
from jax.experimental import pallas as pl
from jax.experimental.pallas import tpu as pltpu
from jax.sharding import PartitionSpec as P

MESH = pl.DeviceIdType.MESH
F32 = jnp.float32
BF16 = jnp.bfloat16
NZ, NX, NY = 8, 4, 4
CHIPS = NZ * NX
LANES = 128
IRREPS = 4
WINDOW = 2
FAR = (2, 1, 3, 0)


def kernel(
    t_hbm, v_hbm, virt_hbm, pair_hbm, out_ref,
    tsrc, virt_ref, pair_ref, recv, vbuf, vf, vmat, tf, tmat, sbuf, s1, msg, fin, move,
    lsem, tsend, trecv, vsem, ssend, srecv, msend, mrecv,
):
    row = lax.axis_index("row")
    col = lax.axis_index("col")
    core = lax.rem(col, 2)
    chip = lax.div(col, 2)
    z = lax.div(chip, NX)
    x = lax.rem(chip, NX)
    other = 1 - core

    for i in range(8):
        pltpu.make_async_copy(t_hbm.at[i], tsrc.at[:, i], lsem.at[0]).start()
    loads = [
        pltpu.make_async_copy(virt_hbm, virt_ref, lsem.at[1]),
        pltpu.make_async_copy(pair_hbm, pair_ref, lsem.at[2]),
        pltpu.make_async_copy(v_hbm, vbuf.at[0], vsem.at[0]),
    ]
    for load in loads:
        load.start()

    def around(dx):
        return lax.rem(x + dx, NX)

    def at(z_index, x_index, core_index, row_index):
        return {"row": row_index, "col": (z_index * NX + x_index) * 2 + core_index}

    def up(dz):
        return lax.rem(z + dz, NZ)

    mates = set()
    for d1 in range(NZ):
        mates |= {(d1, d2, 0, 0) for d2 in range(NX)}
    mates |= {(0, d1, d2, d3) for d1 in range(NX) for d2 in range(2) for d3 in range(NY)}
    mates.remove((0, 0, 0, 0))

    def far(mate):
        dz, dx, dc, dy = mate
        return (-min(dz, NZ - dz) - min(dx, NX - dx) - min(dy, NY - dy), mate)

    mates = sorted(mates, key=far)
    barrier = pltpu.get_barrier_semaphore()
    for dz, dx, dc, dy in mates:
        mate = at(up(dz), around(dx), lax.rem(core + dc, 2), lax.rem(row + dy, NY))
        pl.semaphore_signal(barrier, inc=1, device_id=mate, device_id_type=MESH)
    met = len(mates)
    pltpu.make_async_copy(tsrc, tsrc, lsem.at[0]).wait()
    pl.semaphore_wait(barrier, met)

    def distances(p):
        return 4 - p, p + 4 * lax.div(p + 3, 4)

    def chunk(p, side, dx):
        tz = lax.rem(z + NZ - distances(p)[side], NZ)
        tx = around(dx)
        return pltpu.make_async_remote_copy(
            src_ref=tsrc.at[tz * NX + tx],
            dst_ref=recv.at[p, side * NX + x],
            send_sem=tsend.at[p],
            recv_sem=trecv.at[p],
            device_id=at(tz, tx, core, row),
            device_id_type=MESH,
        )

    def send_phase(p):
        for dx in FAR:
            for side in range(2):
                if (side, dx) == (1, 0):

                    @pl.when(p != 0)
                    def _():
                        chunk(p, side, dx).start()

                else:
                    chunk(p, side, dx).start()

    own_t = pltpu.make_async_copy(tsrc.at[chip], recv.at[0, NX + x], trecv.at[0])
    for p in range(WINDOW):
        send_phase(p)
    own_t.start()
    give_v = pltpu.make_async_remote_copy(
        src_ref=v_hbm, dst_ref=vbuf.at[1], send_sem=vsem.at[1], recv_sem=vsem.at[2],
        device_id=at(z, x, other, row), device_id_type=MESH,
    )
    give_v.start()

    loads[0].wait()
    loads[1].wait()
    labels = virt_ref[...]
    starts = []
    for n in range(1, IRREPS):
        below = jnp.where(labels < n, 1.0, 0.0).astype(F32)
        starts.append(jnp.sum(jnp.sum(below, axis=1, keepdims=True), axis=0, keepdims=True))

    def label_of(place):
        place = place.astype(F32)
        total = jnp.zeros(place.shape, jnp.int32)
        for start in starts:
            total = total + jnp.where(place >= start, 1, 0)
        return total

    irrep_a = label_of(jnp.zeros((1, LANES), jnp.int32))
    irrep_c = virt_ref[pl.ds(row, 1), :]
    irrep_b = label_of(lax.broadcasted_iota(jnp.int32, (512, LANES), 0))

    def lay_v(half, from_core):
        def widen(i, carry):
            rows = pl.ds(pl.multiple_of(i * 512, 512), 512)
            vf[rows, :] = vbuf[half, rows, :].astype(F32)
            return carry

        lax.fori_loop(0, 8, widen, 0)

        for d in range(8):
            place = chip * 16 + from_core * 8 + d
            irrep_d = label_of(jnp.full((1, LANES), 1, jnp.int32) * place)
            want = jnp.bitwise_xor(jnp.bitwise_xor(irrep_d, irrep_c), irrep_a)
            value = vf[pl.ds(d, 512, stride=8), :]
            value = jnp.where(irrep_b == want, value, 0.0)
            value = value.reshape(4, 2, NX, 2, 8, LANES)
            lanes = pl.ds(pl.multiple_of((from_core * 8 + d) * LANES, LANES), LANES)
            for h in range(4):
                for tx in range(NX):
                    for c in range(2):
                        at_row = h * 128 + (tx * 2 + c) * 16
                        vmat[at_row : at_row + 16, lanes] = value[h, :, tx, c].reshape(16, LANES).astype(BF16)

    source = lax.broadcasted_iota(jnp.int32, (LANES, LANES), 0)
    target_lane = lax.broadcasted_iota(jnp.int32, (LANES, LANES), 1)
    origin = lax.rem(lax.div(source, 32) + 4 - lax.div(z, 2), 4)
    target = 64 * lax.div(origin, 2) + 16 * lax.div(lax.rem(source, 32), 8) + 8 * lax.rem(origin, 2) + lax.rem(source, 8)
    move[...] = jnp.where(target == target_lane, 1.0, 0.0).astype(F32)

    loads[2].wait()
    lay_v(0, core)
    give_v.wait()
    lay_v(1, other)

    lane_group = lax.div(lax.broadcasted_iota(jnp.int32, (LANES, LANES), 1), 32)
    me = (row * NX + x) * 2 + core

    def s1_copy(p, side, tx, c):
        plane = up(distances(p)[side])
        return pltpu.make_async_remote_copy(
            src_ref=sbuf.at[p, side, tx * 2 + c],
            dst_ref=s1.at[lax.rem(plane, 2), me],
            send_sem=ssend.at[0],
            recv_sem=srecv.at[0],
            device_id=at(z, tx, c, lax.div(plane, 2)),
            device_id_type=MESH,
        )

    def phase(p, carry):
        @pl.when(p == 0)
        def _():
            pltpu.make_async_copy(recv.at[0, 0:7], recv.at[0, 0:7], tsend.at[0]).wait()

        @pl.when(p != 0)
        def _():
            pltpu.make_async_copy(recv.at[p], recv.at[p], tsend.at[p]).wait()

        @pl.when(p + WINDOW < NY)
        def _():
            send_phase(p + WINDOW)

        pltpu.make_async_copy(recv.at[p], recv.at[p], trecv.at[p]).wait()
        tf[...] = recv[p].reshape(1024, LANES).astype(F32)
        for d in range(16):
            value = tf[pl.ds(d, 64, stride=16), :].astype(BF16)
            for side in range(2):
                for copies in range(4):
                    at_row = side * 128 + copies * 32
                    tmat[at_row : at_row + 32, d * LANES : (d + 1) * LANES] = value[side * 32 : side * 32 + 32]
        product = lax.dot_general(
            vmat[...], tmat[...], (((1,), (1,)), ((), ())), preferred_element_type=F32
        )
        for side in range(2):
            plane = up(distances(p)[side])
            turn = 2 * lax.rem(plane, 2) + core
            packed = product[0:128, side * LANES : (side + 1) * LANES]
            for h in range(1, 4):
                mine = lane_group == lax.rem(h + turn, 4)
                packed = jnp.where(mine, product[h * 128 : h * 128 + 128, side * LANES : (side + 1) * LANES], packed)
            sbuf[p, side] = packed.reshape(8, 16, LANES)
            q = lax.div(plane, 2)
            for dx in FAR:
                for dc in (1, 0):
                    tx = around(dx)
                    c = lax.rem(core + dc, 2)
                    if (dx, dc) == (0, 0):

                        @pl.when(q == row)
                        def _():
                            pltpu.make_async_copy(
                                sbuf.at[p, side, tx * 2 + c], s1.at[lax.rem(plane, 2), me], srecv.at[0]
                            ).start()

                        @pl.when(q != row)
                        def _():
                            s1_copy(p, side, tx, c).start()

                    else:
                        s1_copy(p, side, tx, c).start()
        return carry

    lax.fori_loop(0, NY, phase, 0)

    pltpu.make_async_copy(s1, s1, srecv.at[0]).wait()
    sums = []
    for parity in range(2):
        for c in range(2):
            total = s1[parity, c]
            for i in range(c + 2, 32, 2):
                total = total + s1[parity, i]
            sums.append(total)
    group = lax.div(lax.broadcasted_iota(jnp.int32, (16, LANES), 1), 32)
    for h in range(4):
        merged = sums[0]
        for k in range(1, 4):
            merged = jnp.where(group == (h + k) % 4, sums[k], merged)
        msg[2 * h : 2 * h + 2] = merged.reshape(2, 8, LANES)

    def block(dz):
        return pltpu.make_async_remote_copy(
            src_ref=msg.at[up(dz)], dst_ref=fin.at[z], send_sem=msend.at[0], recv_sem=mrecv.at[0],
            device_id=at(up(dz), x, core, row), device_id_type=MESH,
        )

    for dz in (4, 3, 5, 2, 6, 1, 7):
        block(dz).start()
    pltpu.make_async_copy(msg.at[z], fin.at[z], mrecv.at[0]).start()
    pltpu.make_async_copy(fin, fin, mrecv.at[0]).wait()
    total = fin[0]
    for i in range(1, NZ):
        total = total + fin[i]
    result = lax.dot_general(
        total, move[...], (((1,), (0,)), ((), ())), preferred_element_type=F32, precision=lax.Precision.HIGHEST
    )
    irrep_b8 = label_of(col * 8 + lax.broadcasted_iota(jnp.int32, (8, LANES), 0))
    live = jnp.bitwise_xor(irrep_b8, irrep_a) == pair_ref[pl.ds(row, 1), :]
    out_ref[...] = jnp.where(live, result, 0.0)

    pltpu.make_async_copy(fin.at[0:7], fin.at[0:7], msend.at[0]).wait()
    pltpu.make_async_copy(s1.at[0], s1.at[0], ssend.at[0]).wait()
    pltpu.make_async_copy(s1.at[0, 0:30], s1.at[0, 0:30], ssend.at[0]).wait()


def on_device(amplitudes, integrals, virtual_irrep, pair_irrep):
    v = integrals.reshape(512 * 8, LANES)
    hbm = pl.BlockSpec(memory_space=pltpu.HBM)
    out = pl.pallas_call(
        kernel,
        out_shape=jax.ShapeDtypeStruct((8, LANES), F32),
        in_specs=[hbm, hbm, hbm, hbm],
        out_specs=pl.BlockSpec(memory_space=pltpu.VMEM),
        scratch_shapes=[
            pltpu.VMEM((CHIPS, 8, 16, LANES), BF16),
            pltpu.VMEM((4, LANES), jnp.int32),
            pltpu.VMEM((4, LANES), jnp.int32),
            pltpu.VMEM((4, 8, 8, 16, LANES), BF16),
            pltpu.VMEM((2, 4096, LANES), BF16),
            pltpu.VMEM((4096, LANES), F32),
            pltpu.VMEM((512, 2048), BF16),
            pltpu.VMEM((1024, LANES), F32),
            pltpu.VMEM((256, 2048), BF16),
            pltpu.VMEM((4, 2, 8, 16, LANES), F32),
            pltpu.VMEM((2, 32, 16, LANES), F32),
            pltpu.VMEM((8, 8, LANES), F32),
            pltpu.VMEM((8, 8, LANES), F32),
            pltpu.VMEM((LANES, LANES), F32),
            pltpu.SemaphoreType.DMA((3,)),
            pltpu.SemaphoreType.DMA((4,)),
            pltpu.SemaphoreType.DMA((4,)),
            pltpu.SemaphoreType.DMA((3,)),
            pltpu.SemaphoreType.DMA((1,)),
            pltpu.SemaphoreType.DMA((1,)),
            pltpu.SemaphoreType.DMA((1,)),
            pltpu.SemaphoreType.DMA((1,)),
        ],
        compiler_params=pltpu.CompilerParams(
            collective_id=0, has_side_effects=True, vmem_limit_bytes=63 * 1024 * 1024
        ),
        name="ladder",
    )(amplitudes.reshape(8, CHIPS, 16, LANES), v, virtual_irrep.reshape(4, LANES), pair_irrep.reshape(4, LANES))
    return out.reshape(8, 1, LANES)


def solution(mesh):
    in_specs = (P("col", None, "row"), P(None, None, "col", "row"), P(), P())
    out_specs = P("col", None, "row")
    return jax.shard_map(on_device, mesh=mesh, in_specs=in_specs, out_specs=out_specs, check_vma=False)
```

time: 52.3 us -> 48 us (0.918)
  Pallas kernels: 50.9 us -> 46.3 us
    pallas_call x1, Pallas kernels: 50.9 us -> 46.3 us  [on_device(): pl.pallas_call(kernel, out_shape=jax.ShapeDtypeStruct((8, LANES), F32), i...]
where the time goes in v3:
time: 48 us; the launch traced here: 47.6 us
  Pallas kernels  46.3 us (96%)
  local copies, waits for them, and re-layouts  1.28 us (3%)
    pallas_call x1, Pallas kernels, on_device(): pl.pallas_call(kernel, out_shape=jax.ShapeDtypeStruct((8, LANES), F32), i...  46.3 us
    unnamed x1, local copies, waits for them, and re-layouts  1.28 us

profile of v3, /device:TPU:1, one launch (start us, length us, event | category | flops | bytes accessed | tf_op | source)
XLA Modules:
  0.0 47.6 jit_solution(7964113388318080229)
XLA Ops:
  0.0 46.3 %ladder.1 = f32[8,128]{1,0:T(8,128)} custom-call(bf16[8,32,16,128]{3,2,1,0:T(8,128)(2,1)} %bitcast.7, bf16[4096,128]{1,0:T(8,128)(2,1)} %bitcast.8, s32[4,128]{1,0:T(4,128)} %bitcast.10, s32[4,128]{1,0:T(4,128)} %bitcast.11), custom_call_target="tpu_custom_call" | custom-call | tf_op jit(solution)/shard_map/ladder/pallas_call | solution.py:271
  46.3 1.3 %copy.7 = f32[8,1,128]{2,1,0:T(1,128)} copy(f32[8,1,128]{2,1,0:T(1,128)} %bitcast.9) | data formatting | bytes 8192

commit v4 on v3

--- a/solution.py
+++ b/solution.py
@@ -13,13 +13,14 @@
 LANES = 128
 IRREPS = 4
 WINDOW = 2
+OWN = 2
 FAR = (2, 1, 3, 0)
 
 
 def kernel(
     t_hbm, v_hbm, virt_hbm, pair_hbm, out_ref,
     tsrc, virt_ref, pair_ref, recv, vbuf, vf, vmat, tf, tmat, sbuf, s1, msg, fin, move,
-    lsem, tsend, trecv, vsem, ssend, srecv, msend, mrecv,
+    lsem, tsend, trecv, vsem, ssend, srecv, msend, mrecv, pass_z, pass_y,
 ):
     row = lax.axis_index("row")
     col = lax.axis_index("col")
@@ -29,6 +30,25 @@
     x = lax.rem(chip, NX)
     other = 1 - core
 
+    def around(dx):
+        return lax.rem(x + dx, NX)
+
+    def at(z_index, x_index, core_index, row_index):
+        return {"row": row_index, "col": (z_index * NX + x_index) * 2 + core_index}
+
+    def up(dz):
+        return lax.rem(z + dz, NZ)
+
+    mates = [(dz, dx, 0, 0) for dx in FAR for dz in (1, NZ - 1, 0) if (dz, dx) != (0, 0)]
+    mates += [(0, 0, 0, dy) for dy in (2, 1, 3)] + [(0, 0, 1, 0)]
+    barrier = pltpu.get_barrier_semaphore()
+
+    def mate_at(dz, dx, dc, dy):
+        return at(up(dz), around(dx), lax.rem(core + dc, 2), lax.rem(row + dy, NY))
+
+    for mate in mates:
+        pl.semaphore_signal(barrier, inc=1, device_id=mate_at(*mate), device_id_type=MESH)
+    met = len(mates)
     for i in range(8):
         pltpu.make_async_copy(t_hbm.at[i], tsrc.at[:, i], lsem.at[0]).start()
     loads = [
@@ -38,37 +58,15 @@
     ]
     for load in loads:
         load.start()
-
-    def around(dx):
-        return lax.rem(x + dx, NX)
-
-    def at(z_index, x_index, core_index, row_index):
-        return {"row": row_index, "col": (z_index * NX + x_index) * 2 + core_index}
-
-    def up(dz):
-        return lax.rem(z + dz, NZ)
-
-    mates = set()
-    for d1 in range(NZ):
-        mates |= {(d1, d2, 0, 0) for d2 in range(NX)}
-    mates |= {(0, d1, d2, d3) for d1 in range(NX) for d2 in range(2) for d3 in range(NY)}
-    mates.remove((0, 0, 0, 0))
-
-    def far(mate):
-        dz, dx, dc, dy = mate
-        return (-min(dz, NZ - dz) - min(dx, NX - dx) - min(dy, NY - dy), mate)
-
-    mates = sorted(mates, key=far)
-    barrier = pltpu.get_barrier_semaphore()
-    for dz, dx, dc, dy in mates:
-        mate = at(up(dz), around(dx), lax.rem(core + dc, 2), lax.rem(row + dy, NY))
-        pl.semaphore_signal(barrier, inc=1, device_id=mate, device_id_type=MESH)
-    met = len(mates)
     pltpu.make_async_copy(tsrc, tsrc, lsem.at[0]).wait()
     pl.semaphore_wait(barrier, met)
 
     def distances(p):
-        return 4 - p, p + 4 * lax.div(p + 3, 4)
+        is1 = lax.div(p + 3, 4) - lax.div(p + 2, 4)
+        is2 = lax.div(p + 2, 4) - lax.div(p + 1, 4)
+        is3 = lax.div(p + 1, 4)
+        side_a = 1 + 2 * is1 + 3 * is2 + is3
+        return side_a, (NZ - side_a) * (1 - is2)
 
     def chunk(p, side, dx):
         tz = lax.rem(z + NZ - distances(p)[side], NZ)
@@ -87,16 +85,33 @@
             for side in range(2):
                 if (side, dx) == (1, 0):
 
-                    @pl.when(p != 0)
+                    @pl.when(p != OWN)
                     def _():
                         chunk(p, side, dx).start()
 
                 else:
                     chunk(p, side, dx).start()
 
-    own_t = pltpu.make_async_copy(tsrc.at[chip], recv.at[0, NX + x], trecv.at[0])
-    for p in range(WINDOW):
-        send_phase(p)
+    own_t = pltpu.make_async_copy(tsrc.at[chip], recv.at[OWN, NX + x], trecv.at[OWN])
+    send_phase(0)
+
+    around_z = [(1, 0, 0, 0), (NZ - 1, 0, 0, 0)]
+    in_chip_column = [(0, 0, 0, 2), (0, 0, 0, 1), (0, 0, 0, 3), (0, 0, 1, 0)]
+
+    def pass_on(turn):
+        told = [(pass_z, mate) for mate in around_z]
+        if turn < 2:
+            told += [(pass_y, mate) for mate in in_chip_column]
+        for semaphore, mate in told:
+            pl.semaphore_signal(semaphore.at[turn], inc=1, device_id=mate_at(*mate), device_id_type=MESH)
+        pl.semaphore_wait(pass_z.at[turn], 2)
+        if turn < 2:
+            pl.semaphore_wait(pass_y.at[turn], 4)
+
+    pass_on(0)
+    pass_on(1)
+    send_phase(1)
+    pass_on(2)
     own_t.start()
     give_v = pltpu.make_async_remote_copy(
         src_ref=v_hbm, dst_ref=vbuf.at[1], send_sem=vsem.at[1], recv_sem=vsem.at[2],
@@ -145,11 +160,12 @@
                         at_row = h * 128 + (tx * 2 + c) * 16
                         vmat[at_row : at_row + 16, lanes] = value[h, :, tx, c].reshape(16, LANES).astype(BF16)
 
-    source = lax.broadcasted_iota(jnp.int32, (LANES, LANES), 0)
-    target_lane = lax.broadcasted_iota(jnp.int32, (LANES, LANES), 1)
-    origin = lax.rem(lax.div(source, 32) + 4 - lax.div(z, 2), 4)
-    target = 64 * lax.div(origin, 2) + 16 * lax.div(lax.rem(source, 32), 8) + 8 * lax.rem(origin, 2) + lax.rem(source, 8)
-    move[...] = jnp.where(target == target_lane, 1.0, 0.0).astype(F32)
+    to = lax.broadcasted_iota(jnp.int32, (8, LANES), 1)
+    group_of = lax.rem(2 * lax.div(to, 64) + lax.rem(lax.div(to, 8), 2) + lax.div(z, 2), 4)
+    move[0] = 32 * group_of + 8 * lax.rem(lax.div(to, 16), 4) + lax.rem(to, 8)
+    irrep_b8 = label_of(col * 8 + lax.broadcasted_iota(jnp.int32, (8, LANES), 0))
+    live = jnp.bitwise_xor(irrep_b8, irrep_a) == pair_ref[pl.ds(row, 1), :]
+    move[1] = jnp.where(live, 1, 0)
 
     loads[2].wait()
     lay_v(0, core)
@@ -171,11 +187,11 @@
         )
 
     def phase(p, carry):
-        @pl.when(p == 0)
+        @pl.when(p == OWN)
         def _():
-            pltpu.make_async_copy(recv.at[0, 0:7], recv.at[0, 0:7], tsend.at[0]).wait()
-
-        @pl.when(p != 0)
+            pltpu.make_async_copy(recv.at[p, 0:7], recv.at[p, 0:7], tsend.at[p]).wait()
+
+        @pl.when(p != OWN)
         def _():
             pltpu.make_async_copy(recv.at[p], recv.at[p], tsend.at[p]).wait()
 
@@ -253,12 +269,8 @@
     total = fin[0]
     for i in range(1, NZ):
         total = total + fin[i]
-    result = lax.dot_general(
-        total, move[...], (((1,), (0,)), ((), ())), preferred_element_type=F32, precision=lax.Precision.HIGHEST
-    )
-    irrep_b8 = label_of(col * 8 + lax.broadcasted_iota(jnp.int32, (8, LANES), 0))
-    live = jnp.bitwise_xor(irrep_b8, irrep_a) == pair_ref[pl.ds(row, 1), :]
-    out_ref[...] = jnp.where(live, result, 0.0)
+    result = jnp.take_along_axis(total, move[0], axis=1)
+    out_ref[...] = jnp.where(move[1] == 1, result, 0.0)
 
     pltpu.make_async_copy(fin.at[0:7], fin.at[0:7], msend.at[0]).wait()
     pltpu.make_async_copy(s1.at[0], s1.at[0], ssend.at[0]).wait()
@@ -287,7 +299,7 @@
             pltpu.VMEM((2, 32, 16, LANES), F32),
             pltpu.VMEM((8, 8, LANES), F32),
             pltpu.VMEM((8, 8, LANES), F32),
-            pltpu.VMEM((LANES, LANES), F32),
+            pltpu.VMEM((2, 8, LANES), jnp.int32),
             pltpu.SemaphoreType.DMA((3,)),
             pltpu.SemaphoreType.DMA((4,)),
             pltpu.SemaphoreType.DMA((4,)),
@@ -296,6 +308,8 @@
             pltpu.SemaphoreType.DMA((1,)),
             pltpu.SemaphoreType.DMA((1,)),
             pltpu.SemaphoreType.DMA((1,)),
+            pltpu.SemaphoreType.REGULAR((3,)),
+            pltpu.SemaphoreType.REGULAR((2,)),
         ],
         compiler_params=pltpu.CompilerParams(
             collective_id=0, has_side_effects=True, vmem_limit_bytes=63 * 1024 * 1024

time: 48 us -> 46.9 us (0.977)
  Pallas kernels: 46.3 us -> 45.5 us
    pallas_call x1, Pallas kernels: 46.3 us -> 45.5 us  [on_device(): pl.pallas_call(kernel, out_shape=jax.ShapeDtypeStruct((8, LANES), F32), i...]
where the time goes in v4:
time: 46.9 us; the launch traced here: 46.8 us
  Pallas kernels  45.5 us (97%)
  local copies, waits for them, and re-layouts  1.28 us (3%)
    pallas_call x1, Pallas kernels, on_device(): pl.pallas_call(kernel, out_shape=jax.ShapeDtypeStruct((8, LANES), F32), i...  45.5 us
    unnamed x1, local copies, waits for them, and re-layouts  1.28 us

profile of v4, /device:TPU:1, one launch (start us, length us, event | category | flops | bytes accessed | tf_op | source)
XLA Modules:
  0.0 46.8 jit_solution(6102091146991943937)
XLA Ops:
  0.0 45.5 %ladder.1 = f32[8,128]{1,0:T(8,128)} custom-call(bf16[8,32,16,128]{3,2,1,0:T(8,128)(2,1)} %bitcast.7, bf16[4096,128]{1,0:T(8,128)(2,1)} %bitcast.8, s32[4,128]{1,0:T(4,128)} %bitcast.10, s32[4,128]{1,0:T(4,128)} %bitcast.11), custom_call_target="tpu_custom_call" | custom-call | tf_op jit(solution)/shard_map/ladder/pallas_call | solution.py:283
  45.5 1.3 %copy.7 = f32[8,1,128]{2,1,0:T(1,128)} copy(f32[8,1,128]{2,1,0:T(1,128)} %bitcast.9) | data formatting | bytes 8192

commit v5 on v4

--- a/solution.py
+++ b/solution.py
@@ -312,7 +312,7 @@
             pltpu.SemaphoreType.REGULAR((2,)),
         ],
         compiler_params=pltpu.CompilerParams(
-            collective_id=0, has_side_effects=True, vmem_limit_bytes=63 * 1024 * 1024
+            collective_id=0, has_side_effects=True, vmem_limit_bytes=53 * 1024 * 1024
         ),
         name="ladder",
     )(amplitudes.reshape(8, CHIPS, 16, LANES), v, virtual_irrep.reshape(4, LANES), pair_irrep.reshape(4, LANES))

time: 46.9 us -> 46.4 us (0.989)
  Pallas kernels: 45.5 us -> 44.9 us
    pallas_call x1, Pallas kernels: 45.5 us -> 44.9 us  [on_device(): pl.pallas_call(kernel, out_shape=jax.ShapeDtypeStruct((8, LANES), F32), i...]
    unnamed x1 -> x5, local copies, waits for them, and re-layouts: 1.28 us -> 1.29 us
where the time goes in v5:
time: 46.4 us; the launch traced here: 46.2 us
  Pallas kernels  44.9 us (97%)
  local copies, waits for them, and re-layouts  1.29 us (3%)
    pallas_call x1, Pallas kernels, on_device(): pl.pallas_call(kernel, out_shape=jax.ShapeDtypeStruct((8, LANES), F32), i...  44.9 us
    unnamed x5, local copies, waits for them, and re-layouts  1.29 us

profile of v5, /device:TPU:1, one launch (start us, length us, event | category | flops | bytes accessed | tf_op | source)
XLA Modules:
  0.0 46.2 jit_solution(13379431397266279996)
XLA Ops:
  0.0 0.0 copy-start.1
  0.0 0.0 copy-start
  0.0 0.7 %copy-done.1 = s32[512]{0:T(512)S(1)} copy-done((s32[512]{0:T(512)S(1)}, s32[512]{0:T(512)}, u32[]{:S(2)}) %copy-start.1) | copy-done | bytes 2072
  0.7 0.0 copy-done
  0.7 44.9 %ladder.1 = f32[8,128]{1,0:T(8,128)S(1)} custom-call(bf16[8,32,16,128]{3,2,1,0:T(8,128)(2,1)} %bitcast.10, bf16[4096,128]{1,0:T(8,128)(2,1)} %bitcast.11, s32[4,128]{1,0:T(4,128)S(1)} %bitcast.8, s32[4,128]{1,0:T(4,128)S(1)} %bitcast.9), custom_call_target="tpu_custom_call" | custom-call | tf_op jit(solution)/shard_map/ladder/pallas_call | solution.py:283
  45.6 0.6 %copy.7 = f32[8,1,128]{2,1,0:T(1,128)} copy(f32[8,1,128]{2,1,0:T(1,128)S(1)} %bitcast.7) | data formatting | bytes 8192
Async XLA Ops:
  0.0 0.7 %copy-start.1 = (s32[512]{0:T(512)S(1)}, s32[512]{0:T(512)}, u32[]{:S(2)}) copy-start(s32[512]{0:T(512)} %param.7) | copy-start | bytes 6148
  0.0 0.7 %copy-start = (s32[512]{0:T(512)S(1)}, s32[512]{0:T(512)}, u32[]{:S(2)}) copy-start(s32[512]{0:T(512)} %param.6) | copy-start | bytes 6148

commit v6 on v5

--- a/solution.py
+++ b/solution.py
@@ -12,7 +12,7 @@
 CHIPS = NZ * NX
 LANES = 128
 IRREPS = 4
-WINDOW = 2
+WINDOW = 3
 OWN = 2
 FAR = (2, 1, 3, 0)
 
@@ -112,6 +112,8 @@
     pass_on(1)
     send_phase(1)
     pass_on(2)
+    for p in range(2, WINDOW):
+        send_phase(p)
     own_t.start()
     give_v = pltpu.make_async_remote_copy(
         src_ref=v_hbm, dst_ref=vbuf.at[1], send_sem=vsem.at[1], recv_sem=vsem.at[2],

time: 46.4 us -> 46.3 us (level)
  no operation moved by 1% of the time
where the time goes in v6:
time: 46.3 us; the launch traced here: 46.1 us
  Pallas kernels  44.8 us (97%)
  local copies, waits for them, and re-layouts  1.29 us (3%)
    pallas_call x1, Pallas kernels, on_device(): pl.pallas_call(kernel, out_shape=jax.ShapeDtypeStruct((8, LANES), F32), i...  44.8 us
    unnamed x5, local copies, waits for them, and re-layouts  1.29 us

profile of v6, /device:TPU:1, one launch (start us, length us, event | category | flops | bytes accessed | tf_op | source)
XLA Modules:
  0.0 46.1 jit_solution(4940536031089189227)
XLA Ops:
  0.0 0.0 copy-start.1
  0.0 0.0 copy-start
  0.0 0.7 %copy-done.1 = s32[512]{0:T(512)S(1)} copy-done((s32[512]{0:T(512)S(1)}, s32[512]{0:T(512)}, u32[]{:S(2)}) %copy-start.1) | copy-done | bytes 2072
  0.7 0.0 copy-done
  0.7 44.8 %ladder.1 = f32[8,128]{1,0:T(8,128)S(1)} custom-call(bf16[8,32,16,128]{3,2,1,0:T(8,128)(2,1)} %bitcast.10, bf16[4096,128]{1,0:T(8,128)(2,1)} %bitcast.11, s32[4,128]{1,0:T(4,128)S(1)} %bitcast.8, s32[4,128]{1,0:T(4,128)S(1)} %bitcast.9), custom_call_target="tpu_custom_call" | custom-call | tf_op jit(solution)/shard_map/ladder/pallas_call | solution.py:285
  45.5 0.6 %copy.7 = f32[8,1,128]{2,1,0:T(1,128)} copy(f32[8,1,128]{2,1,0:T(1,128)S(1)} %bitcast.7) | data formatting | bytes 8192
Async XLA Ops:
  0.0 0.7 %copy-start.1 = (s32[512]{0:T(512)S(1)}, s32[512]{0:T(512)}, u32[]{:S(2)}) copy-start(s32[512]{0:T(512)} %param.7) | copy-start | bytes 6148
  0.0 0.7 %copy-start = (s32[512]{0:T(512)S(1)}, s32[512]{0:T(512)}, u32[]{:S(2)}) copy-start(s32[512]{0:T(512)} %param.6) | copy-start | bytes 6148
